TPU v7x, 32 devices: a whole 2x2x4 slice. The times are simulated.
32 devices in a mesh: img: 4 (over z), gx: 2 (over x), gz: 4 (over y, core).
Axes of the slice: x: 2, y: 2, z: 4, core: 2. Of those that a mesh axis runs over, the one named last changes fastest.
Arguments:
- species: float32 [4, 2, 32, 16, 512], P('img', None, 'gx', None, 'gz'), may hold values from -2.5 to 2.5
- diffusion: float32 [2, 32, 16, 512], P(None, 'gx', None, 'gz'), may hold values from 0.1 to 2
- z_inverse: float32 [2, 512, 512], replicated, may hold values from -1 to 1.5
- starts: int32 [4], replicated, may hold values from -1 to 1, as said below
- weights: float32 [4, 4], replicated, may hold values from -0.1 to 1, as said below
Outputs:
- new_string: float32 [4, 2, 32, 16, 512], P('img', None, 'gx', None, 'gz')
Inputs may be any that keep to these rules, and one draw needn't show every extreme that they name: starts[t] is t - 2 or t - 1. Each row holds the cubic Lagrange weights at a point between the second and third of four equally spaced images.
All inputs are finite; a program needn't handle non-finite values.
Results may differ from a plain program's by a relative error of at most 0.00012.
Values sent between devices are 32-bit elements; how exact they have to be, the bound alone decides.
A program may use at most 64 MiB of HBM per device.

v0:
```python
import jax
import jax.numpy as jnp
from jax import lax
from jax.sharding import PartitionSpec as P

STEPS = 4
step_size = 0.05


def with_halo(cells, sides, width):
    for axis, dim in sides:
        count = lax.axis_size(axis)
        ends = count - 1
        head = lax.slice_in_dim(cells, 0, width, axis=dim)
        tail = lax.slice_in_dim(cells, cells.shape[dim] - width, cells.shape[dim], axis=dim)
        cells = jnp.concatenate(
            [
                lax.ppermute(tail, axis, [(i, (i + 1) % count) for i in range(ends)]),
                cells,
                lax.ppermute(head, axis, [((i + 1) % count, i) for i in range(ends)]),
            ],
            axis=dim,
        )
    return cells


def passed_along(value, axis, steps):
    count = lax.axis_size(axis)
    first, last = (max(0, -steps), min(count, count - steps))
    return lax.ppermute(value, axis, [(source, source + steps) for source in range(first, last)])


def reaction(state):
    first = state[0]
    second = state[1]
    return jnp.stack([first - first * first * first - second + 0.2, 0.5 * (first - second)])


def spread_flux(state, padded, coeffs):
    centre = coeffs[:, 1:-1, 1:-1]
    total = (centre + coeffs[:, :-2, 1:-1]) * (padded[:, :-2, 1:-1] - state)
    total = total + (centre + coeffs[:, 2:, 1:-1]) * (padded[:, 2:, 1:-1] - state)
    total = total + (centre + coeffs[:, 1:-1, :-2]) * (padded[:, 1:-1, :-2] - state)
    total = total + (centre + coeffs[:, 1:-1, 2:]) * (padded[:, 1:-1, 2:] - state)
    return 0.5 * total


def local(species, diffusion, z_inverse, starts, weights):
    state = species[0]
    y_widths = ((0, 0), (0, 0), (1, 1), (0, 0))
    coeffs = with_halo(diffusion, (("gx", 1),), 1)
    coeffs = jnp.pad(coeffs, y_widths)
    for repeat in range(STEPS):
        padded = with_halo(state, (("gx", 1),), 1)
        padded = jnp.pad(padded, y_widths)
        source = state + step_size * (reaction(state) + spread_flux(state, padded, coeffs))
        solved = jnp.einsum(
            "sij,sabj->sabi",
            z_inverse,
            lax.all_to_all(source, "gz", split_axis=2, concat_axis=3, tiled=True),
            precision=lax.Precision.HIGHEST,
        )
        state = lax.all_to_all(solved, "gz", split_axis=3, concat_axis=2, tiled=True)
    before_one = passed_along(state, "img", 1)
    before_two = passed_along(state, "img", 2)
    after_one = passed_along(state, "img", -1)
    after_two = passed_along(state, "img", -2)
    images = lax.axis_size("img")
    target = lax.axis_index("img")
    listed = jnp.arange(images, dtype=jnp.int32)
    picked = listed == target
    first_image = jnp.sum(jnp.where(picked, starts, 0))
    my_weights = jnp.sum(jnp.where(picked[:, None], weights, 0.0), axis=0)
    sources = {-2: before_two, -1: before_one, 0: state, 1: after_one, 2: after_two}
    result = None
    for offset in range(-2, 3):
        coef = jnp.zeros((), jnp.float32)
        for place in range(4):
            coef = coef + jnp.where(first_image + place == target + offset, my_weights[place], 0.0)
        term = coef * sources[offset]
        result = term if result is None else result + term
    return result[None]


def solution(mesh):
    return jax.shard_map(
        local,
        mesh=mesh,
        in_specs=(P("img", None, "gx", None, "gz"), P(None, "gx", None, "gz"), P(), P(), P()),
        out_specs=P("img", None, "gx", None, "gz"),
        check_vma=False,
    )
```

profile of v0, /device:TPU:24, one launch (start us, length us, event | category | flops | bytes accessed | tf_op | source)
XLA Modules:
  0.0 201.2 jit_solution(16023715058296012637)
XLA Ops:
  0.0 0.9 fusion.80
  0.9 3.4 %collective-permute-start = (f32[2,1,16,128]{3,1,0,2:T(1,128)S(1)}, f32[2,1,16,128]{3,1,0,2:T(1,128)S(1)}, u32[]{:S(2)}, u32[]{:S(2)}) collective-permute-start(f32[2,1,16,128]{3,1,0,2:T(1,128)S(1)} %copy.23), channel_id=1, source_target_pairs={{0,4},{1,5},{2,6},{3,7},{8,12},{9,13},{10,14},{11,15},{16,20},{17,... | collective-permute-start | bytes 49160 | tf_op jit(solution)/shard_map/ppermute | solution.py:18
  4.4 1.3 collective-permute-start.2
  5.7 1.0 copy.70
  6.7 4.5 %collective-permute-start.1 = (f32[2,1,16,128]{3,1,0,2:T(1,128)S(1)}, f32[2,1,16,128]{3,1,0,2:T(1,128)S(1)}, u32[]{:S(2)}, u32[]{:S(2)}) collective-permute-start(f32[2,1,16,128]{3,1,0,2:T(1,128)S(1)} %get-tuple-element.32), channel_id=1, source_target_pairs={{0,4},{1,5},{2,6},{3,7},{8,12},{9,13},{10,14},{11,15},{16,20},{17,... | collective-permute-start | bytes 49160 | tf_op jit(solution)/shard_map/ppermute | solution.py:18
  11.3 1.3 collective-permute-start.3
  12.6 1.0 fusion.81
  13.7 1.0 copy.25
  14.7 2.2 %collective-permute-done.3 = f32[2,1,16,128]{3,1,0,2:T(1,128)S(1)} collective-permute-done((f32[2,1,16,128]{3,1,0,2:T(1,128)S(1)}, f32[2,1,16,128]{3,1,0,2:T(1,128)S(1)}, u32[]{:S(2)}, u32[]{:S(2)}) %collective-permute-start.3) | collective-permute-done | bytes 16416 | tf_op jit(solution)/shard_map/ppermute | solution.py:20
  17.5 8.6 %all_to_all.144 = f32[2,16,16,128]{3,1,0,2:T(8,128)S(1)} all-to-all(f32[2,16,16,128]{3,1,0,2:T(8,128)S(1)} %get-tuple-element.5), channel_id=1, replica_groups=mesh['img'=4,'gx'=2,'gz'=4] {'gz'}, dimensions={2} | all-to-all | bytes 524288 | tf_op jit(solution)/shard_map/all_to_all | solution.py:60
  26.1 0.9 copy.69
  27.0 1.1 all_to_all.107
  28.0 2.1 %fusion.6 = f32[2,16,4,512]{3,1,2,0:T(8,128)S(1)} fusion(f32[2,16,4,512]{3,1,2,0:T(8,128)S(1)} %all_to_all.107, f32[2,512,512]{2,1,0:T(8,128)S(1)} %copy-done), kind=kOutput, calls=%fused_computation.6 | convolution fusion | flops 402653184 | bytes 2621440 | tf_op jit(solution)/shard_map/sij,sabj->sabi/dot_general | solution.py:57
  30.2 1.7 copy.33
  31.9 3.1 %reshape.265 = f32[4,1,16384]{2,1,0:T(1,128)S(1)} reshape(f32[512,2,4,16]{3,2,1,0:T(4,128)} %bitcast.108) | data formatting | bytes 524288
  35.0 8.4 %all_to_all.145 = f32[4,1,16384]{2,1,0:T(1,128)S(1)} all-to-all(f32[4,1,16384]{2,1,0:T(1,128)S(1)} %reshape.265), channel_id=1, replica_groups=mesh['img'=4,'gx'=2,'gz'=4] {'gz'}, dimensions={0} | all-to-all | bytes 524288 | tf_op jit(solution)/shard_map/all_to_all | solution.py:63
  44.0 1.4 reduce
  45.4 2.9 %reshape.266 = f32[512,2,4,16]{3,2,1,0:T(4,128)} reshape(f32[4,16384]{1,0:T(4,128)S(1)} %reduce) | data formatting | bytes 524288
  48.3 1.8 copy.34
  50.1 2.4 %collective-permute-start.4 = (f32[2,1,16,128]{3,1,0,2:T(1,128)S(1)}, f32[2,1,16,128]{3,1,0,2:T(1,128)S(1)}, u32[]{:S(2)}, u32[]{:S(2)}) collective-permute-start(f32[2,1,16,128]{3,1,0,2:T(1,128)S(1)} %get-tuple-element.24), channel_id=1, source_target_pairs={{0,4},{1,5},{2,6},{3,7},{8,12},{9,13},{10,14},{11,15},{16,20},{17,... | collective-permute-start | bytes 49160 | tf_op jit(solution)/shard_map/ppermute | solution.py:18
  52.5 1.3 collective-permute-start.5
  53.9 4.2 %collective-permute-done.5 = f32[2,1,16,128]{3,1,0,2:T(1,128)S(1)} collective-permute-done((f32[2,1,16,128]{3,1,0,2:T(1,128)S(1)}, f32[2,1,16,128]{3,1,0,2:T(1,128)S(1)}, u32[]{:S(2)}, u32[]{:S(2)}) %collective-permute-start.5) | collective-permute-done | bytes 16416 | tf_op jit(solution)/shard_map/ppermute | solution.py:20
  58.5 8.4 %all_to_all.146 = f32[2,16,16,128]{3,1,0,2:T(8,128)S(1)} all-to-all(f32[2,16,16,128]{3,1,0,2:T(8,128)S(1)} %fusion.40), channel_id=1, replica_groups=mesh['img'=4,'gx'=2,'gz'=4] {'gz'}, dimensions={2} | all-to-all | bytes 524288 | tf_op jit(solution)/shard_map/all_to_all | solution.py:60
  67.0 0.9 copy.68
  67.8 1.1 all_to_all.115
  68.9 2.1 %fusion.4 = f32[2,16,4,512]{3,1,2,0:T(8,128)S(1)} fusion(f32[2,16,4,512]{3,1,2,0:T(8,128)S(1)} %all_to_all.115, f32[2,512,512]{2,1,0:T(8,128)S(1)} %copy-done), kind=kOutput, calls=%fused_computation.4 | convolution fusion | flops 402653184 | bytes 2621440 | tf_op jit(solution)/shard_map/sij,sabj->sabi/dot_general | solution.py:57
  71.0 1.7 copy.36
  72.8 3.1 %reshape.267 = f32[4,1,16384]{2,1,0:T(1,128)S(1)} reshape(f32[512,2,4,16]{3,2,1,0:T(4,128)} %bitcast.110) | data formatting | bytes 524288
  75.8 8.4 %all_to_all.147 = f32[4,1,16384]{2,1,0:T(1,128)S(1)} all-to-all(f32[4,1,16384]{2,1,0:T(1,128)S(1)} %reshape.267), channel_id=1, replica_groups=mesh['img'=4,'gx'=2,'gz'=4] {'gz'}, dimensions={0} | all-to-all | bytes 524288 | tf_op jit(solution)/shard_map/all_to_all | solution.py:63
  84.3 1.4 reduce.1
  85.7 2.9 %reshape.268 = f32[512,2,4,16]{3,2,1,0:T(4,128)} reshape(f32[4,16384]{1,0:T(4,128)S(1)} %reduce.1) | data formatting | bytes 524288
  88.5 1.8 copy.37
  90.4 1.6 collective-permute-start.6
  92.1 1.3 collective-permute-start.7
  93.5 4.2 %collective-permute-done.7 = f32[2,1,16,128]{3,1,0,2:T(1,128)S(1)} collective-permute-done((f32[2,1,16,128]{3,1,0,2:T(1,128)S(1)}, f32[2,1,16,128]{3,1,0,2:T(1,128)S(1)}, u32[]{:S(2)}, u32[]{:S(2)}) %collective-permute-start.7) | collective-permute-done | bytes 16416 | tf_op jit(solution)/shard_map/ppermute | solution.py:20
  98.1 8.4 %all_to_all.148 = f32[2,16,16,128]{3,1,0,2:T(8,128)S(1)} all-to-all(f32[2,16,16,128]{3,1,0,2:T(8,128)S(1)} %fusion.27), channel_id=1, replica_groups=mesh['img'=4,'gx'=2,'gz'=4] {'gz'}, dimensions={2} | all-to-all | bytes 524288 | tf_op jit(solution)/shard_map/all_to_all | solution.py:60
  106.5 0.9 copy.67
  107.4 1.1 all_to_all.123
  108.4 2.1 %fusion.2 = f32[2,16,4,512]{3,1,2,0:T(8,128)S(1)} fusion(f32[2,16,4,512]{3,1,2,0:T(8,128)S(1)} %all_to_all.123, f32[2,512,512]{2,1,0:T(8,128)S(1)} %copy-done), kind=kOutput, calls=%fused_computation.2 | convolution fusion | flops 402653184 | bytes 2621440 | tf_op jit(solution)/shard_map/sij,sabj->sabi/dot_general | solution.py:57
  110.6 1.7 copy.39
  112.3 3.1 %reshape.269 = f32[4,1,16384]{2,1,0:T(1,128)S(1)} reshape(f32[512,2,4,16]{3,2,1,0:T(4,128)} %bitcast.112) | data formatting | bytes 524288
  115.4 8.4 %all_to_all.149 = f32[4,1,16384]{2,1,0:T(1,128)S(1)} all-to-all(f32[4,1,16384]{2,1,0:T(1,128)S(1)} %reshape.269), channel_id=1, replica_groups=mesh['img'=4,'gx'=2,'gz'=4] {'gz'}, dimensions={0} | all-to-all | bytes 524288 | tf_op jit(solution)/shard_map/all_to_all | solution.py:63
  123.8 1.4 reduce.2
  125.2 2.9 %reshape.270 = f32[512,2,4,16]{3,2,1,0:T(4,128)} reshape(f32[4,16384]{1,0:T(4,128)S(1)} %reduce.2) | data formatting | bytes 524288
  128.1 1.8 copy.40
  130.0 1.6 collective-permute-start.8
  131.6 1.3 collective-permute-start.9
  133.1 4.2 %collective-permute-done.9 = f32[2,1,16,128]{3,1,0,2:T(1,128)S(1)} collective-permute-done((f32[2,1,16,128]{3,1,0,2:T(1,128)S(1)}, f32[2,1,16,128]{3,1,0,2:T(1,128)S(1)}, u32[]{:S(2)}, u32[]{:S(2)}) %collective-permute-start.9) | collective-permute-done | bytes 16416 | tf_op jit(solution)/shard_map/ppermute | solution.py:20
  137.6 8.4 %all_to_all.150 = f32[2,16,16,128]{3,1,0,2:T(8,128)S(1)} all-to-all(f32[2,16,16,128]{3,1,0,2:T(8,128)S(1)} %fusion.14), channel_id=1, replica_groups=mesh['img'=4,'gx'=2,'gz'=4] {'gz'}, dimensions={2} | all-to-all | bytes 524288 | tf_op jit(solution)/shard_map/all_to_all | solution.py:60
  146.3 2.1 %fusion = f32[2,16,4,512]{3,1,2,0:T(8,128)S(1)} fusion(f32[2,16,4,512]{3,1,2,0:T(8,128)S(1)} %all_to_all.131, f32[2,512,512]{2,1,0:T(8,128)S(1)} %copy-done), kind=kOutput, calls=%fused_computation | convolution fusion | flops 402653184 | bytes 2621440 | tf_op jit(solution)/shard_map/sij,sabj->sabi/dot_general | solution.py:57
  148.5 1.7 copy.42
  150.2 3.7 %reshape.271 = f32[4,1,16384]{2,1,0:T(1,128)} reshape(f32[512,2,4,16]{3,2,1,0:T(4,128)} %bitcast.114) | data formatting | bytes 524288
  153.9 3.4 %all-to-all-start.7 = ((f32[4,1,16384]{2,1,0:T(1,128)}), f32[4,1,16384]{2,1,0:T(1,128)S(1)}, u32[]{:S(2)}, u32[]{:S(2)}) async-start(f32[4,1,16384]{2,1,0:T(1,128)} %reshape.271), calls=%async_computation.7 | async-start | bytes 524288 | tf_op jit(solution)/shard_map/all_to_all | solution.py:63
  157.4 0.6 select_reduce_fusion.1
  158.0 5.4 %all-to-all-done.7 = f32[4,1,16384]{2,1,0:T(1,128)S(1)} async-done(((f32[4,1,16384]{2,1,0:T(1,128)}), f32[4,1,16384]{2,1,0:T(1,128)S(1)}, u32[]{:S(2)}, u32[]{:S(2)}) %all-to-all-start.7) | async-done | bytes 262176 | tf_op jit(solution)/shard_map/all_to_all | solution.py:63
  163.3 1.4 reduce.3
  164.8 2.9 %reshape.272 = f32[512,2,4,16]{3,2,1,0:T(4,128)} reshape(f32[4,16384]{1,0:T(4,128)S(1)} %reduce.3) | data formatting | bytes 524288
  167.6 1.9 copy.43
  169.5 1.3 collective-permute-start.10
  170.8 1.3 collective-permute-start.11
  172.1 4.6 %collective-permute-start.12 = (f32[2,16,16,128]{3,2,1,0:T(8,128)S(1)}, f32[2,16,16,128]{3,2,1,0:T(8,128)S(1)}, u32[]{:S(2)}, u32[]{:S(2)}) collective-permute-start(f32[2,16,16,128]{3,2,1,0:T(8,128)S(1)} %bitcast.133), channel_id=1, source_target_pairs={{8,0},{16,8},{24,16},{9,1},{17,9},{25,17},{10,2},{18,10},{26,18},{... | collective-permute-start | bytes 786440 | tf_op jit(solution)/shard_map/ppermute | solution.py:30
  176.7 5.5 %collective-permute-start.13 = (f32[2,16,16,128]{3,2,1,0:T(8,128)S(1)}, f32[2,16,16,128]{3,2,1,0:T(8,128)S(1)}, u32[]{:S(2)}, u32[]{:S(2)}) collective-permute-start(f32[2,16,16,128]{3,2,1,0:T(8,128)S(1)} %bitcast.134), channel_id=1, source_target_pairs={{16,0},{24,8},{17,1},{25,9},{18,2},{26,10},{19,3},{27,11},{20,4},{... | collective-permute-start | bytes 786440 | tf_op jit(solution)/shard_map/ppermute | solution.py:30
  186.8 0.7 fusion.83
  200.4 0.8 add_bitcast_fusion
  (45 shorter events, 3.3 us)
Async XLA Ops:
  0.0 28.0 %copy-start = (f32[2,512,512]{2,1,0:T(8,128)S(1)}, f32[2,512,512]{2,1,0:T(8,128)}, u32[]{:S(2)}) copy-start(f32[2,512,512]{2,1,0:T(8,128)} %param.7) | copy-start | bytes 6291460
  0.0 17.1 %copy-start.1 = (f32[2,16,16,128]{3,2,1,0:T(8,128)S(1)}, f32[2,16,16,128]{3,2,1,0:T(8,128)}, u32[]{:S(2)}) copy-start(f32[2,16,16,128]{3,2,1,0:T(8,128)} %param.6) | copy-start | bytes 786436
  0.9 16.1 %collective-permute-start = (f32[2,1,16,128]{3,1,0,2:T(1,128)S(1)}, f32[2,1,16,128]{3,1,0,2:T(1,128)S(1)}, u32[]{:S(2)}, u32[]{:S(2)}) collective-permute-start(f32[2,1,16,128]{3,1,0,2:T(1,128)S(1)} %copy.23), channel_id=1, source_target_pairs={{0,4},{1,5},{2,6},{3,7},{8,12},{9,13},{10,14},{11,15},{16,20},{17,... | collective-permute-start | bytes 49160 | tf_op jit(solution)/shard_map/ppermute | solution.py:18
  4.4 12.6 %collective-permute-start.2 = (f32[2,1,16,128]{3,1,0,2:T(1,128)S(1)}, f32[2,1,16,128]{3,1,0,2:T(1,128)S(1)}, u32[]{:S(2)}, u32[]{:S(2)}) collective-permute-start(f32[2,1,16,128]{3,1,0,2:T(1,128)S(1)} %copy.26), channel_id=1, source_target_pairs={{4,0},{5,1},{6,2},{7,3},{12,8},{13,9},{14,10},{15,11},{20,16},{21,... | collective-permute-start | bytes 49160 | tf_op jit(solution)/shard_map/ppermute | solution.py:20
  6.7 8.0 %collective-permute-start.1 = (f32[2,1,16,128]{3,1,0,2:T(1,128)S(1)}, f32[2,1,16,128]{3,1,0,2:T(1,128)S(1)}, u32[]{:S(2)}, u32[]{:S(2)}) collective-permute-start(f32[2,1,16,128]{3,1,0,2:T(1,128)S(1)} %get-tuple-element.32), channel_id=1, source_target_pairs={{0,4},{1,5},{2,6},{3,7},{8,12},{9,13},{10,14},{11,15},{16,20},{17,... | collective-permute-start | bytes 49160 | tf_op jit(solution)/shard_map/ppermute | solution.py:18
  11.3 5.6 %collective-permute-start.3 = (f32[2,1,16,128]{3,1,0,2:T(1,128)S(1)}, f32[2,1,16,128]{3,1,0,2:T(1,128)S(1)}, u32[]{:S(2)}, u32[]{:S(2)}) collective-permute-start(f32[2,1,16,128]{3,1,0,2:T(1,128)S(1)} %get-tuple-element.33), channel_id=1, source_target_pairs={{4,0},{5,1},{6,2},{7,3},{12,8},{13,9},{14,10},{15,11},{20,16},{21,... | collective-permute-start | bytes 49160 | tf_op jit(solution)/shard_map/ppermute | solution.py:20
  50.1 3.8 %collective-permute-start.4 = (f32[2,1,16,128]{3,1,0,2:T(1,128)S(1)}, f32[2,1,16,128]{3,1,0,2:T(1,128)S(1)}, u32[]{:S(2)}, u32[]{:S(2)}) collective-permute-start(f32[2,1,16,128]{3,1,0,2:T(1,128)S(1)} %get-tuple-element.24), channel_id=1, source_target_pairs={{0,4},{1,5},{2,6},{3,7},{8,12},{9,13},{10,14},{11,15},{16,20},{17,... | collective-permute-start | bytes 49160 | tf_op jit(solution)/shard_map/ppermute | solution.py:18
  52.5 5.6 %collective-permute-start.5 = (f32[2,1,16,128]{3,1,0,2:T(1,128)S(1)}, f32[2,1,16,128]{3,1,0,2:T(1,128)S(1)}, u32[]{:S(2)}, u32[]{:S(2)}) collective-permute-start(f32[2,1,16,128]{3,1,0,2:T(1,128)S(1)} %get-tuple-element.25), channel_id=1, source_target_pairs={{4,0},{5,1},{6,2},{7,3},{12,8},{13,9},{14,10},{15,11},{20,16},{21,... | collective-permute-start | bytes 49160 | tf_op jit(solution)/shard_map/ppermute | solution.py:20
  90.4 3.1 %collective-permute-start.6 = (f32[2,1,16,128]{3,1,0,2:T(1,128)S(1)}, f32[2,1,16,128]{3,1,0,2:T(1,128)S(1)}, u32[]{:S(2)}, u32[]{:S(2)}) collective-permute-start(f32[2,1,16,128]{3,1,0,2:T(1,128)S(1)} %get-tuple-element.18), channel_id=1, source_target_pairs={{0,4},{1,5},{2,6},{3,7},{8,12},{9,13},{10,14},{11,15},{16,20},{17,... | collective-permute-start | bytes 49160 | tf_op jit(solution)/shard_map/ppermute | solution.py:18
  92.1 5.6 %collective-permute-start.7 = (f32[2,1,16,128]{3,1,0,2:T(1,128)S(1)}, f32[2,1,16,128]{3,1,0,2:T(1,128)S(1)}, u32[]{:S(2)}, u32[]{:S(2)}) collective-permute-start(f32[2,1,16,128]{3,1,0,2:T(1,128)S(1)} %get-tuple-element.19), channel_id=1, source_target_pairs={{4,0},{5,1},{6,2},{7,3},{12,8},{13,9},{14,10},{15,11},{20,16},{21,... | collective-permute-start | bytes 49160 | tf_op jit(solution)/shard_map/ppermute | solution.py:20
  130.0 3.1 %collective-permute-start.8 = (f32[2,1,16,128]{3,1,0,2:T(1,128)S(1)}, f32[2,1,16,128]{3,1,0,2:T(1,128)S(1)}, u32[]{:S(2)}, u32[]{:S(2)}) collective-permute-start(f32[2,1,16,128]{3,1,0,2:T(1,128)S(1)} %get-tuple-element.12), channel_id=1, source_target_pairs={{0,4},{1,5},{2,6},{3,7},{8,12},{9,13},{10,14},{11,15},{16,20},{17,... | collective-permute-start | bytes 49160 | tf_op jit(solution)/shard_map/ppermute | solution.py:18
  131.6 5.6 %collective-permute-start.9 = (f32[2,1,16,128]{3,1,0,2:T(1,128)S(1)}, f32[2,1,16,128]{3,1,0,2:T(1,128)S(1)}, u32[]{:S(2)}, u32[]{:S(2)}) collective-permute-start(f32[2,1,16,128]{3,1,0,2:T(1,128)S(1)} %get-tuple-element.13), channel_id=1, source_target_pairs={{4,0},{5,1},{6,2},{7,3},{12,8},{13,9},{14,10},{15,11},{20,16},{21,... | collective-permute-start | bytes 49160 | tf_op jit(solution)/shard_map/ppermute | solution.py:20
  148.5 8.9 %copy-start.3 = (s32[4]{0:T(128)S(1)}, s32[4]{0:T(128)}, u32[]{:S(2)}) copy-start(s32[4]{0:T(128)} %param.8) | copy-start | bytes 52
  153.9 9.4 %all-to-all-start.7 = ((f32[4,1,16384]{2,1,0:T(1,128)}), f32[4,1,16384]{2,1,0:T(1,128)S(1)}, u32[]{:S(2)}, u32[]{:S(2)}) async-start(f32[4,1,16384]{2,1,0:T(1,128)} %reshape.271), calls=%async_computation.7 | async-start | bytes 524288 | tf_op jit(solution)/shard_map/all_to_all | solution.py:63
  164.8 22.0 %copy-start.2 = (f32[4,4]{1,0:T(4,128)S(1)}, f32[4,4]{1,0:T(4,128)}, u32[]{:S(2)}) copy-start(f32[4,4]{1,0:T(4,128)} %param.9) | copy-start | bytes 196
  169.5 30.8 %collective-permute-start.10 = (f32[2,16,16,128]{3,2,1,0:T(8,128)S(1)}, f32[2,16,16,128]{3,2,1,0:T(8,128)S(1)}, u32[]{:S(2)}, u32[]{:S(2)}) collective-permute-start(f32[2,16,16,128]{3,2,1,0:T(8,128)S(1)} %bitcast.131), channel_id=1, source_target_pairs={{0,16},{8,24},{1,17},{9,25},{2,18},{10,26},{3,19},{11,27},{4,20},{... | collective-permute-start | bytes 786440 | tf_op jit(solution)/shard_map/ppermute | solution.py:30
  170.8 29.5 %collective-permute-start.11 = (f32[2,16,16,128]{3,2,1,0:T(8,128)S(1)}, f32[2,16,16,128]{3,2,1,0:T(8,128)S(1)}, u32[]{:S(2)}, u32[]{:S(2)}) collective-permute-start(f32[2,16,16,128]{3,2,1,0:T(8,128)S(1)} %bitcast.132), channel_id=1, source_target_pairs={{0,8},{8,16},{16,24},{1,9},{9,17},{17,25},{2,10},{10,18},{18,26},{... | collective-permute-start | bytes 786440 | tf_op jit(solution)/shard_map/ppermute | solution.py:30
  172.1 28.2 %collective-permute-start.12 = (f32[2,16,16,128]{3,2,1,0:T(8,128)S(1)}, f32[2,16,16,128]{3,2,1,0:T(8,128)S(1)}, u32[]{:S(2)}, u32[]{:S(2)}) collective-permute-start(f32[2,16,16,128]{3,2,1,0:T(8,128)S(1)} %bitcast.133), channel_id=1, source_target_pairs={{8,0},{16,8},{24,16},{9,1},{17,9},{25,17},{10,2},{18,10},{26,18},{... | collective-permute-start | bytes 786440 | tf_op jit(solution)/shard_map/ppermute | solution.py:30
  176.7 23.7 %collective-permute-start.13 = (f32[2,16,16,128]{3,2,1,0:T(8,128)S(1)}, f32[2,16,16,128]{3,2,1,0:T(8,128)S(1)}, u32[]{:S(2)}, u32[]{:S(2)}) collective-permute-start(f32[2,16,16,128]{3,2,1,0:T(8,128)S(1)} %bitcast.134), channel_id=1, source_target_pairs={{16,0},{24,8},{17,1},{25,9},{18,2},{26,10},{19,3},{27,11},{20,4},{... | collective-permute-start | bytes 786440 | tf_op jit(solution)/shard_map/ppermute | solution.py:30
where the time goes:
time: 203 us; the launch traced here: 201 us
  blocking collectives  59.2 us (29%)
  local copies, waits for them, and re-layouts  50.2 us (25%)
  starting transfers between devices  36.1 us (18%)
  waiting for transfers between devices  20.4 us (10%)
  between operations  17.8 us (9%)
  other arithmetic  8.99 us (4%)
  matrix products  8.52 us (4%)
    all_to_all x4, blocking collectives, local(): lax.all_to_all(source, 'gz', split_axis=2, concat_axis=3, tiled=True)  33.9 us
    unnamed x18, local copies, waits for them, and re-layouts  26.4 us
    all_to_all x3, blocking collectives, local(): lax.all_to_all(solved, 'gz', split_axis=3, concat_axis=2, tiled=True)  25.3 us
    ppermute x5, waiting for transfers between devices, with_halo(): lax.ppermute(head, axis, [((i + 1) % count, i) for i in range(ends)])  14.8 us
    ppermute x5, starting transfers between devices, with_halo(): lax.ppermute(tail, axis, [(i, (i + 1) % count) for i in range(ends)])  13.6 us
    ppermute x4, starting transfers between devices, passed_along(): lax.ppermute(value, axis, [(source, source + steps) for source in range(f...  12.6 us
    dot_general x4, matrix products, local(): jnp.einsum('sij,sabj->sabi', z_inverse, lax.all_to_all(source, 'gz', spli...  8.52 us
    all_to_all x5, local copies, waits for them, and re-layouts, local(): lax.all_to_all(solved, 'gz', split_axis=3, concat_axis=2, tiled=True)  7.99 us
  transfers between devices with their start and end apart: 15, of which 8 were waited for; matrix products, arithmetic and copies ran while one was open for 2% of the time, Pallas kernels for 0%

commit v1 on v0

--- a/solution.py
+++ b/solution.py
@@ -2,6 +2,7 @@
 import jax.numpy as jnp
 from jax import lax
 from jax.sharding import PartitionSpec as P
+from jax.lax import all_to_all, axis_size
 
 STEPS = 4
 step_size = 0.05
@@ -54,11 +55,11 @@
         padded = with_halo(state, (("gx", 1),), 1)
         padded = jnp.pad(padded, y_widths)
         source = state + step_size * (reaction(state) + spread_flux(state, padded, coeffs))
+        touch_heaps = lambda shard_in: jnp.concatenate(
+            all_to_all(jnp.stack(jnp.split(shard_in, axis_size("gz"), axis=2)), "gz", 0, 0), axis=3
+        )
         solved = jnp.einsum(
-            "sij,sabj->sabi",
-            z_inverse,
-            lax.all_to_all(source, "gz", split_axis=2, concat_axis=3, tiled=True),
-            precision=lax.Precision.HIGHEST,
+            "sij,sabj->sabi", z_inverse, touch_heaps(source), precision=lax.Precision.HIGHEST
         )
         state = lax.all_to_all(solved, "gz", split_axis=3, concat_axis=2, tiled=True)
     before_one = passed_along(state, "img", 1)

time: 203 us -> 217 us (1.069)
  local copies, waits for them, and re-layouts: 50.2 us -> 61.1 us
  other arithmetic: 8.99 us -> 11.5 us
    slice x1 -> x6, local copies, waits for them, and re-layouts: 0.99 us -> 13.6 us  [reaction(): second = state[1]]
    all_to_all x8 -> x0, local copies, waits for them, and re-layouts: 6.06 us -> none  [local(): lax.all_to_all(source, 'gz', split_axis=2, concat_axis=3, tiled=True)]
    slice x3, local copies, waits for them, and re-layouts: 0.07 us -> 4.63 us  [reaction(): first = state[0]]
where the time goes in v1:
time: 217 us; the launch traced here: 215 us
  local copies, waits for them, and re-layouts  61.1 us (28%)
  blocking collectives  59.2 us (27%)
  starting transfers between devices  36 us (17%)
  waiting for transfers between devices  20.4 us (9%)
  between operations  18.2 us (8%)
  other arithmetic  11.5 us (5%)
  matrix products  8.52 us (4%)
    all_to_all x4, blocking collectives, local(): all_to_all(jnp.stack(jnp.split(shard_in, axis_size('gz'), axis=2)), 'gz',...  33.9 us
    all_to_all x3, blocking collectives, local(): lax.all_to_all(solved, 'gz', split_axis=3, concat_axis=2, tiled=True)  25.3 us
    unnamed x18, local copies, waits for them, and re-layouts  24.3 us
    ppermute x5, waiting for transfers between devices, with_halo(): lax.ppermute(head, axis, [((i + 1) % count, i) for i in range(ends)])  14.9 us
    slice x6, local copies, waits for them, and re-layouts, reaction(): second = state[1]  13.6 us
    ppermute x5, starting transfers between devices, with_halo(): lax.ppermute(tail, axis, [(i, (i + 1) % count) for i in range(ends)])  13.5 us
    ppermute x4, starting transfers between devices, passed_along(): lax.ppermute(value, axis, [(source, source + steps) for source in range(f...  12.6 us
    dot_general x4, matrix products, local(): jnp.einsum('sij,sabj->sabi', z_inverse, touch_heaps(source), precision=la...  8.52 us
  transfers between devices with their start and end apart: 15, of which 8 were waited for; matrix products, arithmetic and copies ran while one was open for 2% of the time, Pallas kernels for 0%

profile of v1, /device:TPU:24, one launch (start us, length us, event | category | flops | bytes accessed | tf_op | source)
XLA Modules:
  0.0 215.0 jit_solution(14838405603117446197)
XLA Ops:
  0.0 0.9 fusion.78
  0.9 3.4 %collective-permute-start = (f32[2,1,16,128]{3,2,1,0:T(8,128)S(1)}, f32[2,1,16,128]{3,2,1,0:T(8,128)S(1)}, u32[]{:S(2)}, u32[]{:S(2)}) collective-permute-start(f32[2,1,16,128]{3,2,1,0:T(8,128)S(1)} %get-tuple-element.43), channel_id=1, source_target_pairs={{0,4},{1,5},{2,6},{3,7},{8,12},{9,13},{10,14},{11,15},{16,20},{17,... | collective-permute-start | bytes 49160 | tf_op jit(solution)/shard_map/ppermute | solution.py:19
  4.3 1.3 collective-permute-start.2
  6.3 4.5 %collective-permute-start.1 = (f32[2,1,16,128]{3,2,1,0:T(8,128)S(1)}, f32[2,1,16,128]{3,2,1,0:T(8,128)S(1)}, u32[]{:S(2)}, u32[]{:S(2)}) collective-permute-start(f32[2,1,16,128]{3,2,1,0:T(8,128)S(1)} %get-tuple-element.46), channel_id=1, source_target_pairs={{0,4},{1,5},{2,6},{3,7},{8,12},{9,13},{10,14},{11,15},{16,20},{17,... | collective-permute-start | bytes 49160 | tf_op jit(solution)/shard_map/ppermute | solution.py:19
  10.9 1.3 collective-permute-start.3
  12.2 1.0 fusion.64
  13.2 1.0 select_maximum_fusion.8
  14.2 2.3 %collective-permute-done.3 = f32[2,1,16,128]{3,2,1,0:T(8,128)S(1)} collective-permute-done((f32[2,1,16,128]{3,2,1,0:T(8,128)S(1)}, f32[2,1,16,128]{3,2,1,0:T(8,128)S(1)}, u32[]{:S(2)}, u32[]{:S(2)}) %collective-permute-start.3) | collective-permute-done | bytes 16416 | tf_op jit(solution)/shard_map/ppermute | solution.py:21
  16.5 1.0 select_maximum_fusion.6
  17.9 8.6 %all_to_all.92 = f32[4,2,16,4,128]{4,3,2,1,0:T(4,128)S(1)} all-to-all(f32[4,2,16,4,128]{4,3,2,1,0:T(4,128)S(1)} %pad_maximum_fusion.10), channel_id=1, replica_groups=mesh['img'=4,'gx'=2,'gz'=4] {'gz'}, dimensions={0} | all-to-all | bytes 524288 | tf_op jit(solution)/shard_map/all_to_all | solution.py:59
  26.8 2.1 fusion.6
  28.9 1.7 copy.21
  30.7 3.1 %reshape.297 = f32[4,1,16384]{2,1,0:T(1,128)S(1)} reshape(f32[512,2,4,16]{3,2,1,0:T(4,128)} %bitcast.110) | data formatting | bytes 524288
  33.7 8.4 %all_to_all.93 = f32[4,1,16384]{2,1,0:T(1,128)S(1)} all-to-all(f32[4,1,16384]{2,1,0:T(1,128)S(1)} %reshape.297), channel_id=1, replica_groups=mesh['img'=4,'gx'=2,'gz'=4] {'gz'}, dimensions={0} | all-to-all | bytes 524288 | tf_op jit(solution)/shard_map/all_to_all | solution.py:64
  42.7 1.4 reduce
  44.1 2.8 %reshape.298 = f32[512,2,4,16]{3,2,1,0:T(4,128)} reshape(f32[4,16384]{1,0:T(4,128)S(1)} %reduce) | data formatting | bytes 524288
  47.0 3.0 %fusion.74 = (f32[1,16,4,4,128]{1,3,0,4,2:T(4,128)}, f32[1,16,4,4,128]{1,3,0,4,2:T(4,128)}) fusion(f32[2,16,4,4,128]{1,3,0,4,2:T(4,128)} %bitcast.104), kind=kLoop, calls=%fused_computation.138 | loop fusion | bytes 524288 | tf_op jit(solution)/shard_map/slice | solution.py:36
  50.0 1.9 copy.22
  51.9 1.5 copy.23
  53.4 1.5 copy.24
  55.0 2.3 %collective-permute-start.4 = (f32[2,1,16,128]{3,2,1,0:T(8,128)S(1)}, f32[2,1,16,128]{3,2,1,0:T(8,128)S(1)}, u32[]{:S(2)}, u32[]{:S(2)}) collective-permute-start(f32[2,1,16,128]{3,2,1,0:T(8,128)S(1)} %get-tuple-element.36), channel_id=1, source_target_pairs={{0,4},{1,5},{2,6},{3,7},{8,12},{9,13},{10,14},{11,15},{16,20},{17,... | collective-permute-start | bytes 49160 | tf_op jit(solution)/shard_map/ppermute | solution.py:19
  57.3 1.3 collective-permute-start.5
  58.7 4.2 %collective-permute-done.5 = f32[2,1,16,128]{3,2,1,0:T(8,128)S(1)} collective-permute-done((f32[2,1,16,128]{3,2,1,0:T(8,128)S(1)}, f32[2,1,16,128]{3,2,1,0:T(8,128)S(1)}, u32[]{:S(2)}, u32[]{:S(2)}) %collective-permute-start.5) | collective-permute-done | bytes 16416 | tf_op jit(solution)/shard_map/ppermute | solution.py:21
  63.3 8.4 %all_to_all.94 = f32[4,2,16,4,128]{4,3,2,1,0:T(4,128)S(1)} all-to-all(f32[4,2,16,4,128]{4,3,2,1,0:T(4,128)S(1)} %pad_maximum_fusion.11), channel_id=1, replica_groups=mesh['img'=4,'gx'=2,'gz'=4] {'gz'}, dimensions={0} | all-to-all | bytes 524288 | tf_op jit(solution)/shard_map/all_to_all | solution.py:59
  72.0 2.1 fusion.4
  74.1 1.7 copy.26
  75.9 3.1 %reshape.299 = f32[4,1,16384]{2,1,0:T(1,128)S(1)} reshape(f32[512,2,4,16]{3,2,1,0:T(4,128)} %bitcast.111) | data formatting | bytes 524288
  78.9 8.4 %all_to_all.95 = f32[4,1,16384]{2,1,0:T(1,128)S(1)} all-to-all(f32[4,1,16384]{2,1,0:T(1,128)S(1)} %reshape.299), channel_id=1, replica_groups=mesh['img'=4,'gx'=2,'gz'=4] {'gz'}, dimensions={0} | all-to-all | bytes 524288 | tf_op jit(solution)/shard_map/all_to_all | solution.py:64
  87.4 1.4 reduce.1
  88.8 2.8 %reshape.300 = f32[512,2,4,16]{3,2,1,0:T(4,128)} reshape(f32[4,16384]{1,0:T(4,128)S(1)} %reduce.1) | data formatting | bytes 524288
  91.6 3.0 %fusion.73 = (f32[1,16,4,4,128]{1,3,0,4,2:T(4,128)}, f32[1,16,4,4,128]{1,3,0,4,2:T(4,128)}) fusion(f32[2,16,4,4,128]{1,3,0,4,2:T(4,128)} %bitcast.106), kind=kLoop, calls=%fused_computation.137 | loop fusion | bytes 524288 | tf_op jit(solution)/shard_map/slice | solution.py:36
  94.6 1.9 copy.27
  96.5 1.5 copy.28
  98.1 1.5 copy.29
  99.6 1.6 collective-permute-start.6
  101.3 1.3 collective-permute-start.7
  102.7 4.2 %collective-permute-done.7 = f32[2,1,16,128]{3,2,1,0:T(8,128)S(1)} collective-permute-done((f32[2,1,16,128]{3,2,1,0:T(8,128)S(1)}, f32[2,1,16,128]{3,2,1,0:T(8,128)S(1)}, u32[]{:S(2)}, u32[]{:S(2)}) %collective-permute-start.7) | collective-permute-done | bytes 16416 | tf_op jit(solution)/shard_map/ppermute | solution.py:21
  107.3 8.4 %all_to_all.96 = f32[4,2,16,4,128]{4,3,2,1,0:T(4,128)S(1)} all-to-all(f32[4,2,16,4,128]{4,3,2,1,0:T(4,128)S(1)} %pad_maximum_fusion.12), channel_id=1, replica_groups=mesh['img'=4,'gx'=2,'gz'=4] {'gz'}, dimensions={0} | all-to-all | bytes 524288 | tf_op jit(solution)/shard_map/all_to_all | solution.py:59
  116.0 2.1 fusion.2
  118.1 1.7 copy.31
  119.8 3.1 %reshape.301 = f32[4,1,16384]{2,1,0:T(1,128)S(1)} reshape(f32[512,2,4,16]{3,2,1,0:T(4,128)} %bitcast.112) | data formatting | bytes 524288
  122.9 8.4 %all_to_all.97 = f32[4,1,16384]{2,1,0:T(1,128)S(1)} all-to-all(f32[4,1,16384]{2,1,0:T(1,128)S(1)} %reshape.301), channel_id=1, replica_groups=mesh['img'=4,'gx'=2,'gz'=4] {'gz'}, dimensions={0} | all-to-all | bytes 524288 | tf_op jit(solution)/shard_map/all_to_all | solution.py:64
  131.3 1.4 reduce.2
  132.7 2.8 %reshape.302 = f32[512,2,4,16]{3,2,1,0:T(4,128)} reshape(f32[4,16384]{1,0:T(4,128)S(1)} %reduce.2) | data formatting | bytes 524288
  135.6 3.0 %fusion.72 = (f32[1,16,4,4,128]{1,3,0,4,2:T(4,128)}, f32[1,16,4,4,128]{1,3,0,4,2:T(4,128)}) fusion(f32[2,16,4,4,128]{1,3,0,4,2:T(4,128)} %bitcast.108), kind=kLoop, calls=%fused_computation.136 | loop fusion | bytes 524288 | tf_op jit(solution)/shard_map/slice | solution.py:36
  138.6 1.9 copy.32
  140.5 1.5 copy.33
  142.0 1.5 copy.34
  143.6 1.6 collective-permute-start.8
  145.2 1.3 collective-permute-start.9
  146.7 4.2 %collective-permute-done.9 = f32[2,1,16,128]{3,2,1,0:T(8,128)S(1)} collective-permute-done((f32[2,1,16,128]{3,2,1,0:T(8,128)S(1)}, f32[2,1,16,128]{3,2,1,0:T(8,128)S(1)}, u32[]{:S(2)}, u32[]{:S(2)}) %collective-permute-start.9) | collective-permute-done | bytes 16416 | tf_op jit(solution)/shard_map/ppermute | solution.py:21
  151.2 8.4 %all_to_all.98 = f32[4,2,16,4,128]{4,3,2,1,0:T(4,128)S(1)} all-to-all(f32[4,2,16,4,128]{4,3,2,1,0:T(4,128)S(1)} %pad_maximum_fusion.13), channel_id=1, replica_groups=mesh['img'=4,'gx'=2,'gz'=4] {'gz'}, dimensions={0} | all-to-all | bytes 524288 | tf_op jit(solution)/shard_map/all_to_all | solution.py:59
  160.0 2.1 fusion
  162.1 1.7 copy.36
  163.8 3.7 %reshape.303 = f32[4,1,16384]{2,1,0:T(1,128)} reshape(f32[512,2,4,16]{3,2,1,0:T(4,128)} %bitcast.113) | data formatting | bytes 524288
  167.5 3.4 %all-to-all-start.7 = ((f32[4,1,16384]{2,1,0:T(1,128)}), f32[4,1,16384]{2,1,0:T(1,128)S(1)}, u32[]{:S(2)}, u32[]{:S(2)}) async-start(f32[4,1,16384]{2,1,0:T(1,128)} %reshape.303), calls=%async_computation.7 | async-start | bytes 524288 | tf_op jit(solution)/shard_map/all_to_all | solution.py:64
  171.6 5.3 %all-to-all-done.7 = f32[4,1,16384]{2,1,0:T(1,128)S(1)} async-done(((f32[4,1,16384]{2,1,0:T(1,128)}), f32[4,1,16384]{2,1,0:T(1,128)S(1)}, u32[]{:S(2)}, u32[]{:S(2)}) %all-to-all-start.7) | async-done | bytes 262176 | tf_op jit(solution)/shard_map/all_to_all | solution.py:64
  176.9 1.4 reduce.3
  178.3 2.8 %reshape.304 = f32[512,2,4,16]{3,2,1,0:T(4,128)} reshape(f32[4,16384]{1,0:T(4,128)S(1)} %reduce.3) | data formatting | bytes 524288
  181.2 1.9 copy.37
  183.1 1.3 collective-permute-start.10
  184.4 1.3 collective-permute-start.11
  185.7 4.6 %collective-permute-start.12 = (f32[2,16,16,128]{3,2,1,0:T(8,128)S(1)}, f32[2,16,16,128]{3,2,1,0:T(8,128)S(1)}, u32[]{:S(2)}, u32[]{:S(2)}) collective-permute-start(f32[2,16,16,128]{3,2,1,0:T(8,128)S(1)} %bitcast.129), channel_id=1, source_target_pairs={{8,0},{16,8},{24,16},{9,1},{17,9},{25,17},{10,2},{18,10},{26,18},{... | collective-permute-start | bytes 786440 | tf_op jit(solution)/shard_map/ppermute | solution.py:31
  190.3 5.5 %collective-permute-start.13 = (f32[2,16,16,128]{3,2,1,0:T(8,128)S(1)}, f32[2,16,16,128]{3,2,1,0:T(8,128)S(1)}, u32[]{:S(2)}, u32[]{:S(2)}) collective-permute-start(f32[2,16,16,128]{3,2,1,0:T(8,128)S(1)} %bitcast.130), channel_id=1, source_target_pairs={{16,0},{24,8},{17,1},{25,9},{18,2},{26,10},{19,3},{27,11},{20,4},{... | collective-permute-start | bytes 786440 | tf_op jit(solution)/shard_map/ppermute | solution.py:31
  (56 shorter events, 6.4 us)
Async XLA Ops:
  0.0 26.8 %copy-start = (f32[2,512,512]{2,1,0:T(8,128)S(1)}, f32[2,512,512]{2,1,0:T(8,128)}, u32[]{:S(2)}) copy-start(f32[2,512,512]{2,1,0:T(8,128)} %param.7) | copy-start | bytes 6291460
  0.0 17.5 %copy-start.1 = (f32[2,16,16,128]{3,2,1,0:T(8,128)S(1)}, f32[2,16,16,128]{3,2,1,0:T(8,128)}, u32[]{:S(2)}) copy-start(f32[2,16,16,128]{3,2,1,0:T(8,128)} %param.6) | copy-start | bytes 786436
  0.0 17.5 %copy-start.2 = (f32[1,2,16,16,128]{4,3,2,1,0:T(8,128)S(1)}, f32[1,2,16,16,128]{4,3,2,1,0:T(8,128)}, u32[]{:S(2)}) copy-start(f32[1,2,16,16,128]{4,3,2,1,0:T(8,128)} %param.5) | copy-start | bytes 786436
  0.9 12.3 %collective-permute-start = (f32[2,1,16,128]{3,2,1,0:T(8,128)S(1)}, f32[2,1,16,128]{3,2,1,0:T(8,128)S(1)}, u32[]{:S(2)}, u32[]{:S(2)}) collective-permute-start(f32[2,1,16,128]{3,2,1,0:T(8,128)S(1)} %get-tuple-element.43), channel_id=1, source_target_pairs={{0,4},{1,5},{2,6},{3,7},{8,12},{9,13},{10,14},{11,15},{16,20},{17,... | collective-permute-start | bytes 49160 | tf_op jit(solution)/shard_map/ppermute | solution.py:19
  4.3 8.9 %collective-permute-start.2 = (f32[2,1,16,128]{3,2,1,0:T(8,128)S(1)}, f32[2,1,16,128]{3,2,1,0:T(8,128)S(1)}, u32[]{:S(2)}, u32[]{:S(2)}) collective-permute-start(f32[2,1,16,128]{3,2,1,0:T(8,128)S(1)} %get-tuple-element.42), channel_id=1, source_target_pairs={{4,0},{5,1},{6,2},{7,3},{12,8},{13,9},{14,10},{15,11},{20,16},{21,... | collective-permute-start | bytes 49160 | tf_op jit(solution)/shard_map/ppermute | solution.py:21
  6.3 7.9 %collective-permute-start.1 = (f32[2,1,16,128]{3,2,1,0:T(8,128)S(1)}, f32[2,1,16,128]{3,2,1,0:T(8,128)S(1)}, u32[]{:S(2)}, u32[]{:S(2)}) collective-permute-start(f32[2,1,16,128]{3,2,1,0:T(8,128)S(1)} %get-tuple-element.46), channel_id=1, source_target_pairs={{0,4},{1,5},{2,6},{3,7},{8,12},{9,13},{10,14},{11,15},{16,20},{17,... | collective-permute-start | bytes 49160 | tf_op jit(solution)/shard_map/ppermute | solution.py:19
  10.9 5.6 %collective-permute-start.3 = (f32[2,1,16,128]{3,2,1,0:T(8,128)S(1)}, f32[2,1,16,128]{3,2,1,0:T(8,128)S(1)}, u32[]{:S(2)}, u32[]{:S(2)}) collective-permute-start(f32[2,1,16,128]{3,2,1,0:T(8,128)S(1)} %get-tuple-element.47), channel_id=1, source_target_pairs={{4,0},{5,1},{6,2},{7,3},{12,8},{13,9},{14,10},{15,11},{20,16},{21,... | collective-permute-start | bytes 49160 | tf_op jit(solution)/shard_map/ppermute | solution.py:21
  55.0 3.7 %collective-permute-start.4 = (f32[2,1,16,128]{3,2,1,0:T(8,128)S(1)}, f32[2,1,16,128]{3,2,1,0:T(8,128)S(1)}, u32[]{:S(2)}, u32[]{:S(2)}) collective-permute-start(f32[2,1,16,128]{3,2,1,0:T(8,128)S(1)} %get-tuple-element.36), channel_id=1, source_target_pairs={{0,4},{1,5},{2,6},{3,7},{8,12},{9,13},{10,14},{11,15},{16,20},{17,... | collective-permute-start | bytes 49160 | tf_op jit(solution)/shard_map/ppermute | solution.py:19
  57.3 5.6 %collective-permute-start.5 = (f32[2,1,16,128]{3,2,1,0:T(8,128)S(1)}, f32[2,1,16,128]{3,2,1,0:T(8,128)S(1)}, u32[]{:S(2)}, u32[]{:S(2)}) collective-permute-start(f32[2,1,16,128]{3,2,1,0:T(8,128)S(1)} %get-tuple-element.37), channel_id=1, source_target_pairs={{4,0},{5,1},{6,2},{7,3},{12,8},{13,9},{14,10},{15,11},{20,16},{21,... | collective-permute-start | bytes 49160 | tf_op jit(solution)/shard_map/ppermute | solution.py:21
  99.6 3.1 %collective-permute-start.6 = (f32[2,1,16,128]{3,2,1,0:T(8,128)S(1)}, f32[2,1,16,128]{3,2,1,0:T(8,128)S(1)}, u32[]{:S(2)}, u32[]{:S(2)}) collective-permute-start(f32[2,1,16,128]{3,2,1,0:T(8,128)S(1)} %get-tuple-element.28), channel_id=1, source_target_pairs={{0,4},{1,5},{2,6},{3,7},{8,12},{9,13},{10,14},{11,15},{16,20},{17,... | collective-permute-start | bytes 49160 | tf_op jit(solution)/shard_map/ppermute | solution.py:19
  101.3 5.6 %collective-permute-start.7 = (f32[2,1,16,128]{3,2,1,0:T(8,128)S(1)}, f32[2,1,16,128]{3,2,1,0:T(8,128)S(1)}, u32[]{:S(2)}, u32[]{:S(2)}) collective-permute-start(f32[2,1,16,128]{3,2,1,0:T(8,128)S(1)} %get-tuple-element.29), channel_id=1, source_target_pairs={{4,0},{5,1},{6,2},{7,3},{12,8},{13,9},{14,10},{15,11},{20,16},{21,... | collective-permute-start | bytes 49160 | tf_op jit(solution)/shard_map/ppermute | solution.py:21
  143.6 3.1 %collective-permute-start.8 = (f32[2,1,16,128]{3,2,1,0:T(8,128)S(1)}, f32[2,1,16,128]{3,2,1,0:T(8,128)S(1)}, u32[]{:S(2)}, u32[]{:S(2)}) collective-permute-start(f32[2,1,16,128]{3,2,1,0:T(8,128)S(1)} %get-tuple-element.20), channel_id=1, source_target_pairs={{0,4},{1,5},{2,6},{3,7},{8,12},{9,13},{10,14},{11,15},{16,20},{17,... | collective-permute-start | bytes 49160 | tf_op jit(solution)/shard_map/ppermute | solution.py:19
  145.2 5.6 %collective-permute-start.9 = (f32[2,1,16,128]{3,2,1,0:T(8,128)S(1)}, f32[2,1,16,128]{3,2,1,0:T(8,128)S(1)}, u32[]{:S(2)}, u32[]{:S(2)}) collective-permute-start(f32[2,1,16,128]{3,2,1,0:T(8,128)S(1)} %get-tuple-element.21), channel_id=1, source_target_pairs={{4,0},{5,1},{6,2},{7,3},{12,8},{13,9},{14,10},{15,11},{20,16},{21,... | collective-permute-start | bytes 49160 | tf_op jit(solution)/shard_map/ppermute | solution.py:21
  162.1 8.8 %copy-start.4 = (s32[4]{0:T(128)S(1)}, s32[4]{0:T(128)}, u32[]{:S(2)}) copy-start(s32[4]{0:T(128)} %param.8) | copy-start | bytes 52
  167.5 9.4 %all-to-all-start.7 = ((f32[4,1,16384]{2,1,0:T(1,128)}), f32[4,1,16384]{2,1,0:T(1,128)S(1)}, u32[]{:S(2)}, u32[]{:S(2)}) async-start(f32[4,1,16384]{2,1,0:T(1,128)} %reshape.303), calls=%async_computation.7 | async-start | bytes 524288 | tf_op jit(solution)/shard_map/all_to_all | solution.py:64
  178.3 22.4 %copy-start.3 = (f32[4,4]{1,0:T(4,128)S(1)}, f32[4,4]{1,0:T(4,128)}, u32[]{:S(2)}) copy-start(f32[4,4]{1,0:T(4,128)} %param.9) | copy-start | bytes 196
  183.1 31.0 %collective-permute-start.10 = (f32[2,16,16,128]{3,2,1,0:T(8,128)S(1)}, f32[2,16,16,128]{3,2,1,0:T(8,128)S(1)}, u32[]{:S(2)}, u32[]{:S(2)}) collective-permute-start(f32[2,16,16,128]{3,2,1,0:T(8,128)S(1)} %bitcast.127), channel_id=1, source_target_pairs={{0,16},{8,24},{1,17},{9,25},{2,18},{10,26},{3,19},{11,27},{4,20},{... | collective-permute-start | bytes 786440 | tf_op jit(solution)/shard_map/ppermute | solution.py:31
  184.4 29.7 %collective-permute-start.11 = (f32[2,16,16,128]{3,2,1,0:T(8,128)S(1)}, f32[2,16,16,128]{3,2,1,0:T(8,128)S(1)}, u32[]{:S(2)}, u32[]{:S(2)}) collective-permute-start(f32[2,16,16,128]{3,2,1,0:T(8,128)S(1)} %bitcast.128), channel_id=1, source_target_pairs={{0,8},{8,16},{16,24},{1,9},{9,17},{17,25},{2,10},{10,18},{18,26},{... | collective-permute-start | bytes 786440 | tf_op jit(solution)/shard_map/ppermute | solution.py:31
  185.7 28.5 %collective-permute-start.12 = (f32[2,16,16,128]{3,2,1,0:T(8,128)S(1)}, f32[2,16,16,128]{3,2,1,0:T(8,128)S(1)}, u32[]{:S(2)}, u32[]{:S(2)}) collective-permute-start(f32[2,16,16,128]{3,2,1,0:T(8,128)S(1)} %bitcast.129), channel_id=1, source_target_pairs={{8,0},{16,8},{24,16},{9,1},{17,9},{25,17},{10,2},{18,10},{26,18},{... | collective-permute-start | bytes 786440 | tf_op jit(solution)/shard_map/ppermute | solution.py:31
  190.3 23.9 %collective-permute-start.13 = (f32[2,16,16,128]{3,2,1,0:T(8,128)S(1)}, f32[2,16,16,128]{3,2,1,0:T(8,128)S(1)}, u32[]{:S(2)}, u32[]{:S(2)}) collective-permute-start(f32[2,16,16,128]{3,2,1,0:T(8,128)S(1)} %bitcast.130), channel_id=1, source_target_pairs={{16,0},{24,8},{17,1},{25,9},{18,2},{26,10},{19,3},{27,11},{20,4},{... | collective-permute-start | bytes 786440 | tf_op jit(solution)/shard_map/ppermute | solution.py:31
